TPU v7x, 256 devices: a whole 4x4x8 slice. The times are simulated.
256 devices in a mesh: dp: 16 (over y, x_hi, core), fsdp: 16 (over x_lo, z).
Axes of the slice: x: 4 (x_hi: 2, x_lo: 2; x = x_hi * 2 + x_lo), y: 4, z: 8, core: 2. Of those that a mesh axis runs over, the one named last changes fastest.
Arguments:
- grads: bfloat16 [16, 1024, 2, 16384], P('dp', 'fsdp'), may hold values from -0.119628906 to 0.119628906
- left_basis_t: bfloat16 [1024, 2, 16384], P('fsdp', None, 'dp'), may hold values from -0.1875 to 0.1875
- right_basis: bfloat16 [1024, 2, 16384], P('fsdp', None, 'dp'), may hold values from -0.1875 to 0.1875
- first_moment: float32 [1024, 2, 16384], P('fsdp', None, 'dp'), may hold values from -0.18 to 0.18
- second_moment: float32 [1024, 2, 16384], P('fsdp', None, 'dp'), may hold values from 0.001 to 0.01
- left_gram: float32 [1024, 2, 16384], P('fsdp', None, 'dp'), may hold values from -1.8 to 1.8
- right_gram: float32 [1024, 2, 16384], P('fsdp', None, 'dp'), may hold values from -1.8 to 1.8
Outputs:
- update: bfloat16 [1024, 2, 16384], P('fsdp')
- new_first: float32 [1024, 2, 16384], P('fsdp', None, 'dp')
- new_second: float32 [1024, 2, 16384], P('fsdp', None, 'dp')
- new_left_gram: float32 [1024, 2, 16384], P('fsdp', None, 'dp')
- new_right_gram: float32 [1024, 2, 16384], P('fsdp', None, 'dp')
All inputs are finite; a program needn't handle non-finite values.
Results may differ from a plain program's by a relative error of at most 0.017.
Values may be sent and summed in bfloat16 or wider, within the bound.
A program may use at most 128 MiB of HBM per device.

v0:
```python
import jax
import jax.numpy as jnp
from jax import lax
from jax.sharding import PartitionSpec as P


def per_device(
    grads, left_basis_t, right_basis, first_moment, second_moment, left_gram, right_gram
):
    own_count = grads.shape[1]
    summed = lax.psum_scatter(
        grads[0].astype(jnp.float32).astype(jnp.bfloat16), "dp", scatter_dimension=2, tiled=True
    )
    offset = lax.axis_index("fsdp") * own_count
    full_grad, complete_right_factor = (
        lax.all_gather(summed, "fsdp", axis=0, tiled=True),
        lax.all_gather(right_basis, "fsdp", axis=0, tiled=True),
    )
    left_new = 0.95 * left_gram + 0.05 * jnp.einsum(
        "ibc,rbc->ibr", summed, full_grad, preferred_element_type=jnp.float32
    )
    grad_columns = lax.dynamic_slice_in_dim(full_grad, offset, own_count, 2)
    right_new = 0.95 * right_gram + 0.05 * jnp.einsum(
        "rbi,rbc->ibc", grad_columns, full_grad, preferred_element_type=jnp.float32
    )
    partial_rotation_step = jnp.einsum(
        "ebr,rbc->ebc", left_basis_t, full_grad, preferred_element_type=jnp.float32
    ).astype(jnp.bfloat16)
    eigen_rotated_grad = jnp.einsum(
        "tnj,jny->tny",
        partial_rotation_step,
        complete_right_factor,
        preferred_element_type=jnp.float32,
    )
    first_new = 0.9 * first_moment + 0.1 * eigen_rotated_grad
    second_new = 0.95 * second_moment + 0.05 * eigen_rotated_grad * eigen_rotated_grad
    normalized_update = (first_new / (jnp.sqrt(second_new) + 1e-08)).astype(jnp.bfloat16)
    projected_blocks = jnp.einsum(
        "pvd,nvd->pvn", normalized_update, complete_right_factor, preferred_element_type=jnp.float32
    ).astype(jnp.bfloat16)
    update_rows = lax.psum_scatter(
        jnp.einsum(
            "ebr,ebc->rbc", left_basis_t, projected_blocks, preferred_element_type=jnp.float32
        ),
        "fsdp",
        scatter_dimension=0,
        tiled=True,
    )
    update = lax.all_gather(update_rows.astype(jnp.bfloat16), "dp", axis=2, tiled=True)
    return (update, first_new, second_new, left_new, right_new)


def solution(mesh):
    in_specs = (
        P("dp", "fsdp", None, None),
        P("fsdp", None, "dp"),
        P("fsdp", None, "dp"),
        P("fsdp", None, "dp"),
        P("fsdp", None, "dp"),
        P("fsdp", None, "dp"),
        P("fsdp", None, "dp"),
    )
    out_specs = (
        P("fsdp", None, None),
        P("fsdp", None, "dp"),
        P("fsdp", None, "dp"),
        P("fsdp", None, "dp"),
        P("fsdp", None, "dp"),
    )
    return jax.shard_map(
        per_device, mesh=mesh, in_specs=in_specs, out_specs=out_specs, check_vma=False
    )
```

profile of v0, /device:TPU:1, one launch (start us, length us, event | category | flops | bytes accessed | tf_op | source)
XLA Modules:
  0.0 485.1 jit_solution(13795475576520292409)
XLA Ops:
  8.0 0.0 reduce-scatter.2.cloned.1.call-start
  8.0 6.5 %copy.59 = bf16[1,64,2,16384]{3,1,2,0:T(8,128)(2,1)} copy(bf16[1,64,2,16384]{3,2,1,0:T(2,128)(2,1)} %param.7) | data formatting | bytes 8388608 | tf_op args[0]
  14.6 0.0 copy-start.7
  14.6 0.0 copy-start.8
  14.6 0.0 copy-start.3
  14.6 0.0 copy-start.5
  14.6 0.0 copy-start.6
  14.6 0.0 reduce-scatter.2.cloned.1.call-update
  14.6 0.0 all-gather.6.cloned.1.call-start
  14.7 0.8 copy-done.7
  15.5 0.8 copy.27
  16.3 0.0 all-gather.6.cloned.1.call-update
  16.3 0.0 all-gather.4.cloned.1.call-start
  16.3 109.4 %reduce-scatter.2.cloned.1.call-done = bf16[64,2,1024]{2,0,1:T(8,128)(2,1)} async-done(((bf16[64,2,16384]{2,0,1:T(8,128)(2,1)}), bf16[64,2,1024]{2,0,1:T(8,128)(2,1)}) %reduce-scatter.2.cloned.1.call-update) | async-done | bytes 262160 | tf_op jit(solution)/shard_map/reduce_scatter | solution.py:11
  125.8 0.0 all-gather.4.cloned.1.call-update
  125.8 0.0 all-gather.8.cloned.1.call-start
  125.8 0.0 copy-done.8
  125.8 0.6 dynamic-slice
  127.1 0.0 all-gather.6.cloned.1.call-done
  127.1 66.6 %all-gather.4.cloned.1.call-done = bf16[1024,2,1024]{2,0,1:T(8,128)(2,1)} async-done(((bf16[64,2,1024]{2,0,1:T(8,128)(2,1)}), bf16[1024,2,1024]{2,0,1:T(8,128)(2,1)}) %all-gather.4.cloned.1.call-update) | async-done | bytes 4194320 | tf_op jit(solution)/shard_map/all_gather | solution.py:16
  193.7 0.0 copy-done.3
  193.7 0.0 copy-done.5
  193.7 0.0 copy-done.6
  193.7 5.3 %fusion.6 = (f32[64,2,1024]{2,0,1:T(8,128)S(1)}, f32[64,2,1024]{2,0,1:T(8,128)S(1)}) fusion(f32[64,2,1024]{2,1,0:T(2,128)S(1)} %copy-done.5, f32[64,2,1024]{2,1,0:T(2,128)S(1)} %copy-done.6, bf16[1024,2,1024]{2,0,1:T(8,128)(2,1)} %all-gather.6.cloned.1.call-done, bf16[1024,2,1024]{2,0,1:T(8,128)(2,1)} %all-gather.4.cloned.1.call-done, ...), kind=kOutput, calls=%fused_computation.14 | convolution fusion | flops 537919488 | bytes 10747904 | tf_op jit(solution)/shard_map/tnj,jny->tny/dot_general | solution.py:29
  199.0 7.9 %convolution_bitcast_fusion = f32[1024,2,1024]{0,2,1:T(8,128)} fusion(bf16[1024,2,1024]{2,0,1:T(8,128)(2,1)} %all-gather.6.cloned.1.call-done, f32[64,2,1024]{2,0,1:T(8,128)S(1)} %get-tuple-element.16, f32[64,2,1024]{2,0,1:T(8,128)S(1)} %get-tuple-element.15, bf16[64,2,1024]{2,1,0:T(2,128)(2,1)S(1)} %copy-done.3), kind=kOutput, calls=%fused_computation.1 | convolution fusion | flops 537395200 | bytes 13893632 | tf_op jit(solution)/shard_map/ebr,ebc->rbc/dot_general | solution.py:42
  206.9 13.3 %copy.30 = f32[1024,2,1024]{2,1,0:T(2,128)} copy(f32[1024,2,1024]{0,2,1:T(8,128)} %convolution_bitcast_fusion) | data formatting | bytes 16777216 | tf_op jit(solution)/shard_map/ebr,ebc->rbc/transpose | solution.py:42
  220.3 0.0 copy-start.2
  220.3 0.0 copy-start.4
  220.3 173.6 %all-reduce.2 = bf16[1024,2,1024]{2,1,0:T(2,128)(2,1)} all-reduce(f32[1024,2,1024]{2,1,0:T(2,128)} %copy.30), channel_id=3, replica_groups=mesh['dp'=16,'fsdp'=16] {'fsdp'}, use_global_device_ids=true, to_apply=%region_1.0.clone | all-reduce | flops 2097152 | bytes 12582912
  393.8 1.8 dynamic-slice_convert_fusion
  395.7 0.0 all-gather.8.cloned.1.call-update
  395.7 0.0 copy-start
  395.7 0.0 copy-start.1
  395.7 1.2 copy.35
  396.9 1.2 copy.34
  398.1 0.0 copy-done.2
  398.1 0.0 copy-done.4
  398.1 3.6 fusion.3
  401.7 1.2 copy.36
  402.9 0.0 copy-done
  402.9 0.0 copy-done.1
  402.9 1.2 fusion.1
  404.1 1.2 copy.37
  405.3 62.0 %all-gather.8.cloned.1.call-done = bf16[64,2,16384]{2,1,0:T(2,128)(2,1)} async-done(((bf16[64,2,1024]{2,1,0:T(2,128)(2,1)}), bf16[64,2,16384]{2,1,0:T(2,128)(2,1)}) %all-gather.8.cloned.1.call-update) | async-done | bytes 4194320 | tf_op jit(solution)/shard_map/all_gather | solution.py:49
  467.3 10.4 %copy.63 = bf16[64,2,16384]{2,1,0:T(2,128)(2,1)} copy(bf16[64,2,16384]{2,1,0:T(2,128)(2,1)} %all-gather.8.cloned.1.call-done) | data formatting | bytes 8388608
Async XLA Ops:
  8.0 117.8 %reduce-scatter.2.cloned.1.call-start = ((), (), s32[]{:S(2)}) async-start(), calls=%async_computation.1 | async-start | bytes 4456448 | tf_op jit(solution)/shard_map/reduce_scatter | solution.py:11
  14.6 0.9 copy-start.7
  14.6 111.3 %copy-start.8 = (u32[256]{0:T(256)S(1)}, u32[256]{0:T(256)}, u32[]{:S(2)}) copy-start(u32[256]{0:T(256)} %constant.23) | copy-start | bytes 3076
  14.6 179.1 %copy-start.3 = (bf16[64,2,1024]{2,1,0:T(2,128)(2,1)S(1)}, bf16[64,2,1024]{2,1,0:T(2,128)(2,1)}, u32[]{:S(2)}) copy-start(bf16[64,2,1024]{2,1,0:T(2,128)(2,1)} %param.8) | copy-start | bytes 786436
  14.6 179.1 %copy-start.5 = (f32[64,2,1024]{2,1,0:T(2,128)S(1)}, f32[64,2,1024]{2,1,0:T(2,128)}, u32[]{:S(2)}) copy-start(f32[64,2,1024]{2,1,0:T(2,128)} %param.11) | copy-start | bytes 1572868
  14.6 179.1 %copy-start.6 = (f32[64,2,1024]{2,1,0:T(2,128)S(1)}, f32[64,2,1024]{2,1,0:T(2,128)}, u32[]{:S(2)}) copy-start(f32[64,2,1024]{2,1,0:T(2,128)} %param.10) | copy-start | bytes 1572868
  14.6 112.5 %all-gather.6.cloned.1.call-start = ((), (), s32[]{:S(2)}) async-start(), calls=%async_computation.3 | async-start | bytes 4456448 | tf_op jit(solution)/shard_map/all_gather | solution.py:17
  16.3 177.4 %all-gather.4.cloned.1.call-start = ((), (), s32[]{:S(2)}) async-start(), calls=%async_computation.2 | async-start | bytes 4456448 | tf_op jit(solution)/shard_map/all_gather | solution.py:16
  125.8 341.5 %all-gather.8.cloned.1.call-start = ((), (), s32[]{:S(2)}) async-start(), calls=%async_computation.4 | async-start | bytes 4456448 | tf_op jit(solution)/shard_map/all_gather | solution.py:49
  220.3 177.8 %copy-start.2 = (bf16[64,2,1024]{2,0,1:T(8,128)(2,1)S(1)}, bf16[64,2,1024]{2,0,1:T(8,128)(2,1)}, u32[]{:S(2)}) copy-start(bf16[64,2,1024]{2,0,1:T(8,128)(2,1)} %reduce-scatter.2.cloned.1.call-done) | copy-start | bytes 786436
  220.3 177.8 %copy-start.4 = (f32[64,2,1024]{2,1,0:T(2,128)S(1)}, f32[64,2,1024]{2,1,0:T(2,128)}, u32[]{:S(2)}) copy-start(f32[64,2,1024]{2,1,0:T(2,128)} %param.12) | copy-start | bytes 1572868
  395.7 7.2 %copy-start = (bf16[1024,2,1024]{2,0,1:T(8,128)(2,1)S(1)}, bf16[1024,2,1024]{2,0,1:T(8,128)(2,1)}, u32[]{:S(2)}) copy-start(bf16[1024,2,1024]{2,0,1:T(8,128)(2,1)} %all-gather.4.cloned.1.call-done) | copy-start | bytes 12582916
  395.7 7.2 %copy-start.1 = (f32[64,2,1024]{2,1,0:T(2,128)S(1)}, f32[64,2,1024]{2,1,0:T(2,128)}, u32[]{:S(2)}) copy-start(f32[64,2,1024]{2,1,0:T(2,128)} %param.13) | copy-start | bytes 1572868
Sparse Core Ops, SparseCore 0:
  14.7 110.9 reduce-scatter.1
  395.8 71.4 all-gather.7
Sparse Core Ops, SparseCore 1:
  17.6 71.5 all-gather.5
  125.9 67.8 all-gather.3
where the time goes:
time: 486 us; the launch traced here: 485 us
  waiting for transfers between devices  238 us (49%)
  blocking collectives  174 us (36%)
  local copies, waits for them, and re-layouts  39.1 us (8%)
  matrix products  18 us (4%)
  between operations  16.2 us (3%)
    unnamed x1, blocking collectives  174 us
    reduce_scatter x1, waiting for transfers between devices, per_device(): lax.psum_scatter(grads[0].astype(jnp.float32).astype(jnp.bfloat16), 'dp',...  109 us
    all_gather x1, waiting for transfers between devices, per_device(): lax.all_gather(summed, 'fsdp', axis=0, tiled=True)  66.6 us
    all_gather x1, waiting for transfers between devices, per_device(): lax.all_gather(update_rows.astype(jnp.bfloat16), 'dp', axis=2, tiled=True)  62 us
    unnamed x26, local copies, waits for them, and re-layouts  24 us
    transpose x1, local copies, waits for them, and re-layouts, per_device(): jnp.einsum('ebr,ebc->rbc', left_basis_t, projected_blocks, preferred_elem...  13.3 us
  transfers between devices with their start and end apart: 4, of which 3 were waited for; matrix products, arithmetic and copies ran while one was open for 2% of the time, Pallas kernels for 0%

commit v1 on v0

v1 whole, which is shorter than its diff:
```python
import jax
import jax.numpy as jnp
from jax import lax
from jax.experimental import pallas as pl
from jax.experimental.pallas import tpu as pltpu
from jax.sharding import PartitionSpec as P

MESH = pl.DeviceIdType.MESH
F32, BF16 = jnp.float32, jnp.bfloat16
NCOPY = 200
H = 2
W = 1024 // H
PIECE = 1024 // H
CONTRACT_LAST = (((1,), (1,)), ((), ()))


def rows_view(x):
    i, b, n = x.shape
    return x.reshape(i, b, n // 128, 128).transpose(0, 2, 1, 3)


class Peers:
    def __init__(self):
        dp, fs = lax.axis_index("dp"), lax.axis_index("fsdp")
        self.y, self.xh, self.c = lax.div(dp, 4), lax.rem(lax.div(dp, 2), 2), lax.rem(dp, 2)
        self.xl, self.z = lax.div(fs, 8), lax.rem(fs, 8)

    def at(self, dy=0, dxh=0, dc=0, dxl=0, dz=0):
        y, xh, c = lax.rem(self.y + dy, 4), lax.rem(self.xh + dxh, 2), lax.rem(self.c + dc, 2)
        xl, z = lax.rem(self.xl + dxl, 2), lax.rem(self.z + dz, 8)
        return ((y * 2 + xh) * 2 + c, xl * 8 + z)


def kernel(
    g, lt, qr, m1, m2,
    out, rot, pleft, pright,
    in_bf, mom_in, own, other, summed, y_recv, x_send, x_recv, acc,
    q_split, q_full, l_split, l_rows, l_perm, l_all, l_t,
    g_full, mom, mom_recv, y_rot, n_buf, m_full, r_buf, r_recv, pl_buf, pl_recv, pr_buf, pr_recv,
    g_cols, up_send, up_recv, pack, up_piece,
    ss, rs, ls,
):
    k = Peers()
    y, xh, c, xl, z = k.y, k.xh, k.c, k.xl, k.z
    count = [0, 0]
    unsent = []

    def remote(src, dst, peer):
        n = count[0]
        count[0] += 1
        copy = pltpu.make_async_remote_copy(
            src, dst, ss.at[n], rs.at[n], device_id=peer, device_id_type=MESH
        )
        unsent.append(copy)
        return copy

    def send(src, dst, peer):
        copy = remote(src, dst, peer)
        copy.start()
        return copy

    def local(src, dst):
        n = count[1]
        count[1] += 1
        copy = pltpu.make_async_copy(src, dst, ls.at[n])
        copy.start()
        return copy

    partners = (
        [k.at(dc=1), k.at(dxl=1), k.at(dxh=1), k.at(dxh=1, dxl=1)]
        + [k.at(dy=o) for o in (1, 2, 3)]
        + [k.at(dz=o) for o in range(1, 8)]
    )
    barrier = pltpu.get_barrier_semaphore()
    for peer in partners:
        pl.semaphore_signal(barrier, inc=1, device_id=peer, device_id_type=MESH)

    load_q = local(qr, in_bf.at[0])
    load_l = local(lt, in_bf.at[1])
    load_own = [local(g.at[pl.ds(q * 32, 32), :, c], own.at[q]) for q in range(2)]
    load_m = [local(m1, mom_in.at[0]), local(m2, mom_in.at[1])]

    def split_bf(src, dst):
        acc[...] = src[...].reshape(1024, 128).astype(F32)
        for b in range(2):
            for t in range(8):
                dst[b, :, pl.ds(t * 128, 128)] = acc[pl.ds(t * 2 + b, 64, stride=16), :].astype(BF16)

    class ZGather:
        def __init__(self, ref):
            self.ref, self.copies = ref, {}

        def start(self, s, j):
            for d in (1, -1):
                if s == 4 and j != (d == -1):
                    continue
                at = self.ref(lax.rem(xl + j, 2), lax.rem(z - d * (s - 1) + 8, 8))
                self.copies[s, j, d] = send(at, at, k.at(dz=d % 8))

        def arrive(self, s, j):
            for d in (1, -1):
                if (s, j, d) in self.copies:
                    self.copies[s, j, d].wait_recv()

        def step(self, s, j):
            self.arrive(s, j)
            if s < 4:
                self.start(s + 1, j)

    zq = ZGather(lambda j, zz: q_full.at[j, zz])
    zg = [
        ZGather(lambda j, zz, q=q: g_full.at[j, zz, pl.ds(q * 32, 32), :]) for q in range(2)
    ]
    zm = [ZGather(lambda j, zz, h=h: m_full.at[h, j, zz]) for h in range(H)]

    load_q.wait()
    split_bf(in_bf.at[0], q_split)
    q_full[xl, z] = q_split[xl]
    pl.semaphore_wait(barrier, len(partners))

    core = [send(g.at[pl.ds(q * 32, 32), :, 1 - c], other.at[q], k.at(dc=1)) for q in range(2)]
    xq = send(q_split.at[1 - xl], q_full.at[xl, z], k.at(dxl=1))
    zq.start(1, 0)
    load_l.wait()
    split_bf(in_bf.at[1], l_split)
    xt = send(l_split.at[1 - xl], l_rows.at[xl], k.at(dxl=1))
    l_rows[xl] = l_split[xl]

    y_copies = {}

    def core_sum(q):
        load_own[q].wait()
        core[q].wait_recv()
        for o in (2, 1, 3, 0):
            yy = lax.rem(y + o, 4)

            @pl.loop(0, 8)
            def _(i):
                at = (q, pl.ds(i * 4, 4), pl.ds(yy * 2, 2))
                total = own[at].astype(F32) + other[at].astype(F32)
                summed[q, yy, pl.ds(i * 4, 4)] = total.astype(BF16)

            if o:
                y_copies[q, o] = send(summed.at[q, yy], y_recv.at[q, o - 1], k.at(dy=o))

    x_copies = {}

    def y_sum(q):
        for o in (1, 2, 3):
            y_copies[q, o].wait_recv()

        @pl.loop(0, 8)
        def _(i):
            at = pl.ds(i * 4, 4)
            total = summed[q, y, at].astype(F32)
            for o in range(3):
                total += y_recv[q, o, at].astype(F32)
            acc[pl.ds(i * 128, 128), :] = total.reshape(128, 128)

        for e in range(2):
            for b in range(2):
                for t in range(8):
                    x_send[q, e, b, :, pl.ds(t * 128, 128)] = acc[
                        pl.ds(e * 16 + t * 2 + b, 32, stride=32), :
                    ].astype(BF16)
        for n, (dh, dl) in enumerate(((1, 1), (1, 0), (0, 1))):
            x_copies[q, n] = send(
                x_send.at[q, lax.rem(xh + dh, 2), lax.rem(xl + dl, 2)],
                x_recv.at[q, n],
                k.at(dxh=dh, dxl=dl),
            )

    def x_sum(q):
        at = pl.ds(q * 32, 32)
        x_copies[q, 1].wait_recv()
        g_full[xl, z, at] = (
            x_send[q, xh, xl].astype(F32) + x_recv[q, 1].astype(F32)
        ).astype(BF16)
        zg[q].start(1, 0)
        x_copies[q, 0].wait_recv()
        x_copies[q, 2].wait_recv()
        g_full[1 - xl, z, at] = (x_recv[q, 0].astype(F32) + x_recv[q, 2].astype(F32)).astype(BF16)
        zg[q].start(1, 1)

    core_sum(0)
    xq.wait_recv()
    zq.start(1, 1)
    zq.step(1, 0)
    core_sum(1)
    zq.step(1, 1)

    for n in range(2):
        load_m[n].wait()
        for b in range(2):
            for t in range(8):
                mom[n, b, :, pl.ds(t * 128, 128)] = mom_in[n, pl.ds(t * 2 + b, 64, stride=16), :]
    xm = send(mom.at[:, 1 - xl], mom_recv, k.at(dxl=1))
    zq.step(2, 0)

    xt.wait_recv()
    low = lax.broadcasted_iota(jnp.int32, (64, 128), 1) < 64
    for j in range(2):
        for zz in range(8):
            a = l_rows[j, :, pl.ds(zz // 2 * 128, 128)].astype(F32)
            b = l_rows[j, :, pl.ds((4 + zz // 2) * 128, 128)].astype(F32)
            if zz % 2:
                a = pltpu.roll(a, 64, 1)
            else:
                b = pltpu.roll(b, 64, 1)
            l_perm[zz, j] = jnp.where(low, a, b).astype(BF16)
    l_copies = []
    for o in range(1, 8):
        zz = lax.rem(z + o, 8)
        l_copies.append(send(l_perm.at[zz], l_all.at[:, z], k.at(dz=o)))
    l_all[:, z] = l_perm[z]

    zq.step(2, 1)
    zq.step(3, 0)
    y_sum(0)
    zq.step(3, 1)
    zq.step(4, 0)
    x_sum(0)
    zq.step(4, 1)
    zg[0].step(1, 0)
    zg[0].step(1, 1)
    zg[0].step(2, 0)
    zg[0].step(2, 1)
    y_sum(1)
    zg[0].step(3, 0)
    zg[0].step(3, 1)
    x_sum(1)
    zg[0].step(4, 0)
    zg[0].step(4, 1)
    for copy in l_copies:
        copy.wait_recv()
    l_t[...] = l_all[...].reshape(1024, 128).astype(F32).T.astype(BF16)
    for s in range(1, 5):
        zg[1].step(s, 0)
        zg[1].step(s, 1)

    def dot(a, b):
        return jnp.dot(a, b, preferred_element_type=F32)

    left = l_rows[...].reshape(128, 1024)
    for t in range(4):
        cols = pl.ds(t * 256, 256)
        y_rot[:, cols] = dot(left, g_full[:, :, :, cols].reshape(1024, 256)).astype(BF16)
    xm.wait_recv()
    for t in range(4):
        cols = pl.ds(t * 256, 256)
        r = dot(y_rot[...], q_full[:, :, :, cols].reshape(1024, 256)).reshape(2, 64, 256)
        r_buf[:, :, cols] = r
        for j in range(2):
            first = mom[0, xl, :, cols] if j == 0 else mom_recv[0, :, cols]
            second = mom[1, xl, :, cols] if j == 0 else mom_recv[1, :, cols]
            rj = r_buf[lax.rem(xl + j, 2), :, cols]
            first = 0.9 * first + 0.1 * rj
            second = 0.95 * second + 0.05 * rj * rj
            n_buf[lax.rem(xl + j, 2), :, cols] = (first / (jnp.sqrt(second) + 1e-8)).astype(BF16)
    normal = n_buf[...].reshape(128, 1024)
    for h in range(H):
        per = 16 // H
        for t in range(W // 256):
            slabs = q_full[...].reshape(1024, 1024)[h * W + t * 256 : h * W + (t + 1) * 256]
            part = lax.dot_general(normal, slabs, CONTRACT_LAST, preferred_element_type=F32)
            part = part.astype(BF16).reshape(2, 64, 256)
            for j in range(2):
                m_full[h, j, z, :, pl.ds(t * 256, 256)] = part[j]
        zm[h].start(1, 0)
        zm[h].start(1, 1)

    xr = send(r_buf.at[1 - xl], r_recv, k.at(dxl=1))

    def left_gram():
        rows = g_full[:, z].reshape(128, 1024)
        for t in range(4):
            slabs = g_full[...].reshape(1024, 1024)[t * 256 : (t + 1) * 256]
            part = lax.dot_general(rows, slabs, CONTRACT_LAST, preferred_element_type=F32)
            pl_buf[:, :, pl.ds(t * 256, 256)] = part.reshape(2, 64, 256)

    def right_gram():
        half = lax.div(z, 2)
        odd = lax.rem(z, 2) == 1
        wide = lax.broadcasted_iota(jnp.int32, (128, 128), 1) < 64

        for j in range(2):
            for n in range(4):
                at = pl.ds(n * 2, 2)
                a = g_full[j, at, :, pl.ds(pl.multiple_of(half * 128, 128), 128)]
                b = g_full[j, at, :, pl.ds(pl.multiple_of((half + 4) * 128, 128), 128)]
                a, b = a.reshape(128, 128).astype(F32), b.reshape(128, 128).astype(F32)
                a = jnp.where(odd, pltpu.roll(a, 64, 1), a)
                b = jnp.where(odd, b, pltpu.roll(b, 64, 1))
                g_cols[:, pl.ds((j * 4 + n) * 128, 128)] = jnp.where(wide, a, b).T.astype(BF16)
        cols = g_cols[...]
        for t in range(4):
            at = pl.ds(t * 256, 256)
            pr_buf[:, :, at] = dot(cols, g_full[:, :, :, at].reshape(1024, 256)).reshape(2, 64, 256)

    up_copies = {}
    left_t = l_t

    def update(h):
        for t in range(W // 256):
            cols = pl.ds(t * 256, 256)
            part = dot(left_t[...], m_full[h, :, :, :, cols].reshape(1024, 256))
            up_send[h, :, :, cols] = part.astype(BF16).reshape(2, 64, 256)
        up_copies[h] = send(up_send.at[h, 1 - xl], up_recv.at[h], k.at(dxl=1))

    gathers = []

    class Gather:
        def __init__(self, h):
            self.h, self.got = h, {}

        def place(self, dy, dxh, dc, half=None):
            yy, hh, cc = lax.rem(y + dy, 4), lax.rem(xh + dxh, 2), lax.rem(c + dc, 2)
            ref = out.at[(yy * 2 + hh) * 2 + cc, self.h]
            if half is not None:
                ref = ref.at[pl.ds(half * (PIECE // 2), PIECE // 2)]
            return ref

        def push(self, name, src, peer, half=None):
            dst = src
            if src is None:
                src, dst = up_piece.at[self.h], self.place(0, 0, 0)
            self.got[name] = send(src, dst, peer)

        def begin(self):
            self.keep = local(up_piece.at[self.h], self.place(0, 0, 0))
            self.push("x", None, k.at(dxh=1))
            self.push((0, 1), None, k.at(dy=1))
            self.push((0, 3), None, k.at(dy=3))
            self.push((0, 0, "c"), None, k.at(dc=1))

        def x_arrive(self):
            self.got["x"].wait_recv()
            at = self.place(0, 1, 0)
            self.push((1, 1), at, k.at(dy=1))
            self.push((1, 3), at, k.at(dy=3))
            self.push((1, 0, "c"), at, k.at(dc=1))

        def relay(self, e):
            self.got[e, 1].wait_recv()
            self.push((e, 2, 0), self.place(3, e, 0, 0), k.at(dy=1))
            self.push((e, 1, "c"), self.place(3, e, 0), k.at(dc=1))
            self.got[e, 3].wait_recv()
            self.push((e, 2, 1), self.place(1, e, 0, 1), k.at(dy=3))
            self.push((e, 3, "c"), self.place(1, e, 0), k.at(dc=1))

        def finish(self, e):
            self.got[e, 2, 0].wait_recv()
            self.got[e, 2, 1].wait_recv()
            self.push((e, 2, "c"), self.place(2, e, 0), k.at(dc=1))

        def end(self):
            for e in range(2):
                for o in range(4):
                    self.got[e, o, "c"].wait_recv()
            self.keep.wait()

    gathers = [Gather(h) for h in range(H)]

    def pack_up(h):
        up_copies[h].wait_recv()
        n = W // 128
        for b in range(2):
            for t in range(n):
                cols = pl.ds(t * 128, 128)
                mine, theirs = up_send[h, xl, :, cols], up_recv[h, :, cols]
                piece = jnp.where(xl == b, mine.astype(F32), theirs.astype(F32))
                pack[pl.ds(t * 2 + b, 64, stride=2 * n), :] = piece
        up_piece[h] = pack[...].astype(BF16)
        gathers[h].begin()

    left_gram()
    xl_copy = send(pl_buf.at[1 - xl], pl_recv, k.at(dxl=1))
    zm[0].step(1, 0)
    zm[0].step(1, 1)
    zm[1].step(1, 0)
    zm[1].step(1, 1)
    right_gram()
    xr_copy = send(pr_buf.at[1 - xl], pr_recv, k.at(dxl=1))
    for s in (2, 3):
        for h in range(H):
            zm[h].step(s, 0)
            zm[h].step(s, 1)
    zm[0].step(4, 0)
    zm[0].step(4, 1)
    update(0)
    zm[1].step(4, 0)
    zm[1].step(4, 1)
    pack_up(0)
    update(1)
    gathers[0].x_arrive()
    pack_up(1)
    gathers[0].relay(0)

    def weave(dst, buf, received):
        for b in range(2):
            for t in range(8):
                cols = pl.ds(t * 128, 128)
                dst[pl.ds(t * 2 + b, 64, stride=16), :] = jnp.where(
                    xl == b, buf[xl, :, cols], received[:, cols]
                )

    xr.wait_recv()
    weave(rot, r_buf, r_recv)
    gathers[1].x_arrive()
    gathers[0].relay(1)
    gathers[0].finish(0)
    xl_copy.wait_recv()
    weave(pleft, pl_buf, pl_recv)
    gathers[1].relay(0)
    gathers[0].finish(1)
    xr_copy.wait_recv()
    weave(pright, pr_buf, pr_recv)
    gathers[1].relay(1)
    gathers[1].finish(0)
    gathers[1].finish(1)
    gathers[0].end()
    gathers[1].end()
    for copy in unsent:
        copy.wait_send()


def per_device(grads, left_basis_t, right_basis, first, second, left_gram, right_gram):
    g = rows_view(grads[0]).reshape(64, 8, 2, 16, 128)
    lt, qr = (rows_view(a).reshape(64, 16, 128) for a in (left_basis_t, right_basis))
    m1, m2, lg, rg = (rows_view(a).reshape(1024, 128) for a in (first, second, left_gram, right_gram))
    any_spec, vmem = pl.BlockSpec(memory_space=pl.ANY), pl.BlockSpec(memory_space=pltpu.VMEM)
    shape = jax.ShapeDtypeStruct
    v = pltpu.VMEM
    out, rot, pleft, pright = pl.pallas_call(
        kernel,
        out_shape=[shape((16, H, PIECE, 128), BF16)] + [shape((1024, 128), F32)] * 3,
        in_specs=[any_spec] * 5,
        out_specs=[any_spec] + [vmem] * 3,
        scratch_shapes=[
            v((2, 64, 16, 128), BF16),
            v((2, 1024, 128), F32),
            v((2, 32, 8, 16, 128), BF16),
            v((2, 32, 8, 16, 128), BF16),
            v((2, 4, 32, 2, 16, 128), BF16),
            v((2, 3, 32, 2, 16, 128), BF16),
            v((2, 2, 2, 32, 1024), BF16),
            v((2, 3, 32, 1024), BF16),
            v((1024, 128), F32),
            v((2, 64, 1024), BF16),
            v((2, 8, 64, 1024), BF16),
            v((2, 64, 1024), BF16),
            v((2, 64, 1024), BF16),
            v((8, 2, 64, 128), BF16),
            v((2, 8, 64, 128), BF16),
            v((128, 1024), BF16),
            v((2, 8, 64, 1024), BF16),
            v((2, 2, 64, 1024), F32),
            v((2, 64, 1024), F32),
            v((128, 1024), BF16),
            v((2, 64, 1024), BF16),
            v((H, 2, 8, 64, W), BF16),
            v((2, 64, 1024), F32),
            v((64, 1024), F32),
            v((2, 64, 1024), F32),
            v((64, 1024), F32),
            v((2, 64, 1024), F32),
            v((64, 1024), F32),
            v((128, 1024), BF16),
            v((H, 2, 64, W), BF16),
            v((H, 64, W), BF16),
            v((PIECE, 128), F32),
            v((H, PIECE, 128), BF16),
            pltpu.SemaphoreType.DMA((NCOPY,)),
            pltpu.SemaphoreType.DMA((NCOPY,)),
            pltpu.SemaphoreType.DMA((16,)),
        ],
        compiler_params=pltpu.CompilerParams(
            collective_id=0, has_side_effects=True, vmem_limit_bytes=40 << 20
        ),
        name="soap",
    )(g, lt, qr, m1, m2)
    n1 = 0.9 * m1 + 0.1 * rot
    n2 = 0.95 * m2 + 0.05 * rot * rot
    nl = 0.95 * lg + 0.05 * pleft
    nr = 0.95 * rg + 0.05 * pright
    update = out.reshape(16, H, 64, PIECE // 64, 128).transpose(2, 0, 1, 3, 4)
    update = update.reshape(64, 128, 2, 128).transpose(0, 2, 1, 3).reshape(64, 2, 16384)

    def back(a):
        return a.reshape(64, 8, 2, 128).transpose(0, 2, 1, 3).reshape(64, 2, 1024)

    return update, back(n1), back(n2), back(nl), back(nr)


def solution(mesh):
    sharded = P("fsdp", None, "dp")
    return jax.shard_map(
        per_device,
        mesh=mesh,
        in_specs=(P("dp", "fsdp", None, None),) + (sharded,) * 6,
        out_specs=(P("fsdp", None, None),) + (sharded,) * 4,
        check_vma=False,
    )
```

time: 486 us -> 141 us (0.29)
  waiting for transfers between devices: 238 us -> 0 us
  blocking collectives: 174 us -> 0 us
  Pallas kernels: 0 us -> 118 us
  local copies, waits for them, and re-layouts: 39.1 us -> 19 us
  matrix products: 18 us -> 0 us
  between operations: 16.2 us -> 0.69 us
    unnamed x1 -> x0, blocking collectives: 174 us -> none
    all_gather x3 -> x0, waiting for transfers between devices: 129 us -> none  [the longest x1 66.6 us: per_device(): lax.all_gather(summed, 'fsdp', axis=0, tiled=True)]
    pallas_call x0 -> x1, Pallas kernels: none -> 118 us  [per_device(): pl.pallas_call(kernel, out_shape=[shape((16, H, PIECE, 128), BF16)] + [sh...]
    reduce_scatter x1 -> x0, waiting for transfers between devices: 109 us -> none  [per_device(): lax.psum_scatter(grads[0].astype(jnp.float32).astype(jnp.bfloat16), 'dp',...]
    dot_general x4 -> x0, matrix products: 18 us -> none  [the longest x1 7.92 us: per_device(): jnp.einsum('ebr,ebc->rbc', left_basis_t, projected_blocks, preferred_elem...]
    transpose x1 -> x0, local copies, waits for them, and re-layouts: 13.3 us -> none  [per_device(): jnp.einsum('ebr,ebc->rbc', left_basis_t, projected_blocks, preferred_elem...]
    unnamed x26 -> x20, local copies, waits for them, and re-layouts: 24 us -> 17.8 us
  transfers between devices with their start and end apart: 4 -> 0, of which waited for: 3 -> 0; matrix products, arithmetic and copies ran while one was open for 2% -> 0% of each run, Pallas kernels for 0% -> 0%
where the time goes in v1:
time: 141 us; the launch traced here: 140 us
  Pallas kernels  118 us (84%)
  local copies, waits for them, and re-layouts  19 us (13%)
  other arithmetic  2.62 us (2%)
    pallas_call x1, Pallas kernels, per_device(): pl.pallas_call(kernel, out_shape=[shape((16, H, PIECE, 128), BF16)] + [sh...  118 us
    unnamed x20, local copies, waits for them, and re-layouts  17.8 us

profile of v1, /device:TPU:1, one launch (start us, length us, event | category | flops | bytes accessed | tf_op | source)
XLA Modules:
  0.0 140.3 jit_solution(9875074245829180946)
XLA Ops:
  0.6 0.0 copy-start
  0.6 2.2 %copy-done = bf16[1,64,2,16384]{3,2,1,0:T(2,128)(2,1)S(1)} copy-done((bf16[1,64,2,16384]{3,2,1,0:T(2,128)(2,1)S(1)}, bf16[1,64,2,16384]{3,2,1,0:T(2,128)(2,1)}, u32[]{:S(2)}) %copy-start) | copy-done | bytes 4194328
  2.8 0.0 copy-start.1
  2.8 1.0 copy-done.1
  3.9 0.0 copy-start.3
  3.9 1.0 copy-done.3
  4.9 0.0 copy-start.5
  4.9 0.9 copy-done.5
  5.9 0.0 copy-start.6
  5.9 0.9 copy-done.6
  6.8 118.0 %soap.1 = (bf16[16,2,512,128]{3,2,1,0:T(8,128)(2,1)S(1)}, f32[1024,128]{1,0:T(8,128)S(1)}, f32[1024,128]{1,0:T(8,128)S(1)}, f32[1024,128]{1,0:T(8,128)S(1)}) custom-call(bf16[64,8,2,16,128]{4,3,2,1,0:T(8,128)(2,1)S(1)} %bitcast.63, bf16[64,16,128]{2,1,0:T(8,128)(2,1)S(1)} %bitcast.69, bf16[64,16,128]{2,1,0:T(8,128)(2,1)S(1)} %bitcast.70, ...), custom_call_target="tpu_custom_call" | custom-call | tf_op jit(solution)/shard_map/soap/pallas_call | solution.py:434
  124.8 1.2 copy.40
  126.0 4.7 %copy.49 = bf16[64,2,128,128]{3,2,1,0:T(8,128)(2,1)} copy(bf16[64,2,128,128]{3,0,1,2:T(8,128)(2,1)S(1)} %bitcast.71) | data formatting | bytes 8388608
  130.7 0.0 copy-start.7
  130.7 0.0 copy-start.2
  130.7 0.0 copy-start.4
  130.7 7.0 %reshape.102 = bf16[64,2,16384]{2,1,0:T(2,128)(2,1)} reshape(bf16[64,2,128,128]{3,2,1,0:T(8,128)(2,1)} %copy.49) | data formatting | bytes 8388608
  137.7 0.0 copy-start.8
  137.7 0.0 copy-done.7
  137.7 0.3 broadcast_multiply_fusion
  137.9 0.0 copy-done.2
  138.0 0.0 copy-done.4
  138.0 1.2 fusion
  139.2 0.0 copy-done.8
  139.2 0.3 broadcast_multiply_fusion.1
  139.5 0.9 multiply_add_fusion.1
Async XLA Ops:
  0.6 2.2 %copy-start = (bf16[1,64,2,16384]{3,2,1,0:T(2,128)(2,1)S(1)}, bf16[1,64,2,16384]{3,2,1,0:T(2,128)(2,1)}, u32[]{:S(2)}) copy-start(bf16[1,64,2,16384]{3,2,1,0:T(2,128)(2,1)} %param.7) | copy-start | bytes 12582916
  2.8 1.0 copy-start.1
  3.9 1.0 copy-start.3
  4.9 0.9 copy-start.5
  5.9 0.9 copy-start.6
  130.7 7.0 %copy-start.7 = (f32[64,2,1024]{2,1,0:T(2,128)S(1)}, f32[64,2,1024]{2,1,0:T(2,128)}, u32[]{:S(2)}) copy-start(f32[64,2,1024]{2,1,0:T(2,128)} %param.13) | copy-start | bytes 1572868
  130.7 7.3 %copy-start.2 = (f32[64,2,1024]{2,1,0:T(2,128)S(1)}, f32[64,2,1024]{2,1,0:T(2,128)}, u32[]{:S(2)}) copy-start(f32[64,2,1024]{2,1,0:T(2,128)} %param.10) | copy-start | bytes 1572868
  130.7 7.3 %copy-start.4 = (f32[64,2,1024]{2,1,0:T(2,128)S(1)}, f32[64,2,1024]{2,1,0:T(2,128)}, u32[]{:S(2)}) copy-start(f32[64,2,1024]{2,1,0:T(2,128)} %param.11) | copy-start | bytes 1572868
  137.7 1.5 %copy-start.8 = (f32[64,2,1024]{2,1,0:T(2,128)S(1)}, f32[64,2,1024]{2,1,0:T(2,128)}, u32[]{:S(2)}) copy-start(f32[64,2,1024]{2,1,0:T(2,128)} %param.12) | copy-start | bytes 1572868

commit v2 on v1

--- a/solution.py
+++ b/solution.py
@@ -32,9 +32,9 @@
 
 
 def kernel(
-    g, lt, qr, m1, m2,
-    out, rot, pleft, pright,
-    in_bf, mom_in, own, other, summed, y_recv, x_send, x_recv, acc,
+    g, lt, qr, m1, m2, lg, rg,
+    out, new_first_out, new_second_out, new_left_out, new_right_out,
+    new_first, new_second, new_left, new_right, gram_in, in_bf, mom_in, own, other, summed, y_recv, x_send, x_recv, acc,
     q_split, q_full, l_split, l_rows, l_perm, l_all, l_t,
     g_full, mom, mom_recv, y_rot, n_buf, m_full, r_buf, r_recv, pl_buf, pl_recv, pr_buf, pr_recv,
     g_cols, up_send, up_recv, pack, up_piece,
@@ -79,6 +79,7 @@
     load_l = local(lt, in_bf.at[1])
     load_own = [local(g.at[pl.ds(q * 32, 32), :, c], own.at[q]) for q in range(2)]
     load_m = [local(m1, mom_in.at[0]), local(m2, mom_in.at[1])]
+    load_g = [local(lg, gram_in.at[0]), local(rg, gram_in.at[1])]
 
     def split_bf(src, dst):
         acc[...] = src[...].reshape(1024, 128).astype(F32)
@@ -396,47 +397,100 @@
     pack_up(1)
     gathers[0].relay(0)
 
-    def weave(dst, buf, received):
+    def woven(buf, received, b, t):
+        cols = pl.ds(t * 128, 128)
+        return jnp.where(xl == b, buf[xl, :, cols], received[:, cols])
+
+    def new_moments():
         for b in range(2):
             for t in range(8):
-                cols = pl.ds(t * 128, 128)
-                dst[pl.ds(t * 2 + b, 64, stride=16), :] = jnp.where(
-                    xl == b, buf[xl, :, cols], received[:, cols]
-                )
+                at = pl.ds(t * 2 + b, 64, stride=16)
+                r = woven(r_buf, r_recv, b, t)
+                new_first[at, :] = 0.9 * mom_in[0, at, :] + 0.1 * r
+                new_second[at, :] = 0.95 * mom_in[1, at, :] + 0.05 * r * r
+
+    def new_gram(dst, n, buf, received):
+        load_g[n].wait()
+        for b in range(2):
+            for t in range(8):
+                at = pl.ds(t * 2 + b, 64, stride=16)
+                dst[at, :] = 0.95 * gram_in[n, at, :] + 0.05 * woven(buf, received, b, t)
 
     xr.wait_recv()
-    weave(rot, r_buf, r_recv)
+    new_moments()
+    results = [local(new_first, new_first_out), local(new_second, new_second_out)]
     gathers[1].x_arrive()
     gathers[0].relay(1)
     gathers[0].finish(0)
     xl_copy.wait_recv()
-    weave(pleft, pl_buf, pl_recv)
+    new_gram(new_left, 0, pl_buf, pl_recv)
+    results.append(local(new_left, new_left_out))
     gathers[1].relay(0)
     gathers[0].finish(1)
     xr_copy.wait_recv()
-    weave(pright, pr_buf, pr_recv)
+    new_gram(new_right, 1, pr_buf, pr_recv)
+    results.append(local(new_right, new_right_out))
     gathers[1].relay(1)
     gathers[1].finish(0)
     gathers[1].finish(1)
     gathers[0].end()
     gathers[1].end()
+    for copy in results:
+        copy.wait()
     for copy in unsent:
         copy.wait_send()
+
+
+def write_out(part, n1, n2, nl, nr, update, o1, o2, ol, orr, held, whole, rest, sems):
+    loads, copies = [], []
+    for n in range(4):
+        at = pl.ds(n * 4, 4)
+        loads.append(pltpu.make_async_copy(part.at[at], held.at[at], sems.at[n]))
+        loads[-1].start()
+    for n, src in enumerate((n1, n2, nl, nr)):
+        loads.append(pltpu.make_async_copy(src, rest.at[n], sems.at[4 + n]))
+        loads[-1].start()
+    for n in range(4):
+        loads[n].wait()
+
+        @pl.loop(n * 4, n * 4 + 4)
+        def _(d):
+            for r in range(4):
+                rows = [
+                    held[d, h, pl.ds(r * 128, 128), :].astype(F32).reshape(16, 8, 128)
+                    for h in range(H)
+                ]
+                whole[pl.ds(r * 16, 16), d] = jnp.concatenate(rows, axis=1).astype(BF16)
+
+        at = (slice(None), pl.ds(n * 4, 4))
+        copies.append(pltpu.make_async_copy(whole.at[at], update.at[at], sems.at[8 + n]))
+        copies[-1].start()
+    for n, dst in enumerate((o1, o2, ol, orr)):
+        loads[4 + n].wait()
+        copies.append(pltpu.make_async_copy(rest.at[n], dst, sems.at[n]))
+        copies[-1].start()
+    for copy in copies:
+        copy.wait()
 
 
 def per_device(grads, left_basis_t, right_basis, first, second, left_gram, right_gram):
     g = rows_view(grads[0]).reshape(64, 8, 2, 16, 128)
     lt, qr = (rows_view(a).reshape(64, 16, 128) for a in (left_basis_t, right_basis))
     m1, m2, lg, rg = (rows_view(a).reshape(1024, 128) for a in (first, second, left_gram, right_gram))
-    any_spec, vmem = pl.BlockSpec(memory_space=pl.ANY), pl.BlockSpec(memory_space=pltpu.VMEM)
+    hbm = pl.BlockSpec(memory_space=pl.ANY)
     shape = jax.ShapeDtypeStruct
     v = pltpu.VMEM
-    out, rot, pleft, pright = pl.pallas_call(
+    done = pl.pallas_call(
         kernel,
-        out_shape=[shape((16, H, PIECE, 128), BF16)] + [shape((1024, 128), F32)] * 3,
-        in_specs=[any_spec] * 5,
-        out_specs=[any_spec] + [vmem] * 3,
+        out_shape=[shape((16, H, PIECE, 128), BF16)] + [shape((1024, 128), F32)] * 4,
+        in_specs=[hbm] * 7,
+        out_specs=[hbm] * 5,
         scratch_shapes=[
+            v((1024, 128), F32),
+            v((1024, 128), F32),
+            v((1024, 128), F32),
+            v((1024, 128), F32),
+            v((2, 1024, 128), F32),
             v((2, 64, 16, 128), BF16),
             v((2, 1024, 128), F32),
             v((2, 32, 8, 16, 128), BF16),
@@ -475,21 +529,30 @@
             pltpu.SemaphoreType.DMA((16,)),
         ],
         compiler_params=pltpu.CompilerParams(
-            collective_id=0, has_side_effects=True, vmem_limit_bytes=40 << 20
+            collective_id=0, has_side_effects=True, vmem_limit_bytes=56 << 20
         ),
         name="soap",
-    )(g, lt, qr, m1, m2)
-    n1 = 0.9 * m1 + 0.1 * rot
-    n2 = 0.95 * m2 + 0.05 * rot * rot
-    nl = 0.95 * lg + 0.05 * pleft
-    nr = 0.95 * rg + 0.05 * pright
-    update = out.reshape(16, H, 64, PIECE // 64, 128).transpose(2, 0, 1, 3, 4)
+    )(g, lt, qr, m1, m2, lg, rg)
+    update, *rest = pl.pallas_call(
+        write_out,
+        out_shape=[shape((64, 16, 16, 128), BF16)] + [shape((1024, 128), F32)] * 4,
+        in_specs=[hbm] * 5,
+        out_specs=[hbm] * 5,
+        scratch_shapes=[
+            v((16, H, PIECE, 128), BF16),
+            v((64, 16, 16, 128), BF16),
+            v((4, 1024, 128), F32),
+            pltpu.SemaphoreType.DMA((12,)),
+        ],
+        compiler_params=pltpu.CompilerParams(vmem_limit_bytes=56 << 20),
+        name="write_out",
+    )(*done)
     update = update.reshape(64, 128, 2, 128).transpose(0, 2, 1, 3).reshape(64, 2, 16384)
 
     def back(a):
         return a.reshape(64, 8, 2, 128).transpose(0, 2, 1, 3).reshape(64, 2, 1024)
 
-    return update, back(n1), back(n2), back(nl), back(nr)
+    return (update, *(back(a) for a in rest))
 
 
 def solution(mesh):

time: 141 us -> 125 us (0.89)
  local copies, waits for them, and re-layouts: 19 us -> 0 us
  Pallas kernels: 118 us -> 124 us
  other arithmetic: 2.62 us -> 0 us
    unnamed x20 -> x0, local copies, waits for them, and re-layouts: 17.8 us -> none
    pallas_call x0 -> x1, Pallas kernels: none -> 4.78 us  [per_device(): pl.pallas_call(write_out, out_shape=[shape((64, 16, 16, 128), BF16)] + [s...]
    add x2 -> x0, other arithmetic: 2.08 us -> none  [the longest x1 1.22 us: per_device(): n2 = 0.95 * m2 + 0.05 * rot * rot]
where the time goes in v2:
time: 125 us
  Pallas kernels  124 us (99%)
    pallas_call x1, Pallas kernels, per_device(): pl.pallas_call(kernel, out_shape=[shape((16, H, PIECE, 128), BF16)] + [sh...  119 us
    pallas_call x1, Pallas kernels, per_device(): pl.pallas_call(write_out, out_shape=[shape((64, 16, 16, 128), BF16)] + [s...  4.78 us

profile of v2, /device:TPU:1, one launch (start us, length us, event | category | flops | bytes accessed | tf_op | source)
XLA Modules:
  0.0 124.8 jit_solution(13367442506146840953)
XLA Ops:
  0.6 119.4 %soap.1 = (bf16[16,2,512,128]{3,2,1,0:T(8,128)(2,1)}, f32[1024,128]{1,0:T(8,128)}, f32[1024,128]{1,0:T(8,128)}, f32[1024,128]{1,0:T(8,128)}, f32[1024,128]{1,0:T(8,128)}) custom-call(bf16[64,8,2,16,128]{4,3,2,1,0:T(8,128)(2,1)} %bitcast.60, bf16[64,16,128]{2,1,0:T(8,128)(2,1)} %bitcast.65, bf16[64,16,128]{2,1,0:T(8,128)(2,1)} %bitcast.66, ...), custom_call_target="tpu_custom_call" | custom-call | tf_op jit(solution)/shard_map/soap/pallas_call | solution.py:483
  120.0 4.8 %write_out.1 = (bf16[64,16,16,128]{3,2,1,0:T(8,128)(2,1)}, f32[1024,128]{1,0:T(8,128)}, f32[1024,128]{1,0:T(8,128)}, f32[1024,128]{1,0:T(8,128)}, f32[1024,128]{1,0:T(8,128)}) custom-call(bf16[16,2,512,128]{3,2,1,0:T(8,128)(2,1)} %get-tuple-element.15.part, f32[1024,128]{1,0:T(8,128)} %get-tuple-element.16.n1, f32[1024,128]{1,0:T(8,128)} %get-tuple-element.17.n2, ...), custom_call_target="tpu_custom_call" | custom-call | tf_op jit(solution)/shard_map/write_out/pallas_call | solution.py:536

commit v3 on v2

--- a/solution.py
+++ b/solution.py
@@ -7,8 +7,8 @@
 
 MESH = pl.DeviceIdType.MESH
 F32, BF16 = jnp.float32, jnp.bfloat16
-NCOPY = 200
-H = 2
+NCOPY = 256
+H = 4
 W = 1024 // H
 PIECE = 1024 // H
 CONTRACT_LAST = (((1,), (1,)), ((), ()))
@@ -34,7 +34,7 @@
 def kernel(
     g, lt, qr, m1, m2, lg, rg,
     out, new_first_out, new_second_out, new_left_out, new_right_out,
-    new_first, new_second, new_left, new_right, gram_in, in_bf, mom_in, own, other, summed, y_recv, x_send, x_recv, acc,
+    new_first, new_second, new_left, new_right, gram_in, in_bf, mom_in, own, other, summed, y_recv, y_relay, x_send, x_recv, acc,
     q_split, q_full, l_split, l_rows, l_perm, l_all, l_t,
     g_full, mom, mom_recv, y_rot, n_buf, m_full, r_buf, r_recv, pl_buf, pl_recv, pr_buf, pr_recv,
     g_cols, up_send, up_recv, pack, up_piece,
@@ -108,25 +108,23 @@
             if s < 4:
                 self.start(s + 1, j)
 
+        def steps(self, s):
+            self.step(s, 0)
+            self.step(s, 1)
+
     zq = ZGather(lambda j, zz: q_full.at[j, zz])
     zg = [
         ZGather(lambda j, zz, q=q: g_full.at[j, zz, pl.ds(q * 32, 32), :]) for q in range(2)
     ]
     zm = [ZGather(lambda j, zz, h=h: m_full.at[h, j, zz]) for h in range(H)]
 
+    pl.semaphore_wait(barrier, len(partners))
+    core = [send(g.at[pl.ds(q * 32, 32), :, 1 - c], other.at[q], k.at(dc=1)) for q in range(2)]
     load_q.wait()
     split_bf(in_bf.at[0], q_split)
     q_full[xl, z] = q_split[xl]
-    pl.semaphore_wait(barrier, len(partners))
-
-    core = [send(g.at[pl.ds(q * 32, 32), :, 1 - c], other.at[q], k.at(dc=1)) for q in range(2)]
     xq = send(q_split.at[1 - xl], q_full.at[xl, z], k.at(dxl=1))
     zq.start(1, 0)
-    load_l.wait()
-    split_bf(in_bf.at[1], l_split)
-    xt = send(l_split.at[1 - xl], l_rows.at[xl], k.at(dxl=1))
-    l_rows[xl] = l_split[xl]
-
     y_copies = {}
 
     def core_sum(q):
@@ -138,31 +136,52 @@
             @pl.loop(0, 8)
             def _(i):
                 at = (q, pl.ds(i * 4, 4), pl.ds(yy * 2, 2))
-                total = own[at].astype(F32) + other[at].astype(F32)
-                summed[q, yy, pl.ds(i * 4, 4)] = total.astype(BF16)
-
-            if o:
-                y_copies[q, o] = send(summed.at[q, yy], y_recv.at[q, o - 1], k.at(dy=o))
+                total = (own[at].astype(F32) + other[at].astype(F32)).astype(BF16)
+                for e in range(2):
+                    summed[q, yy, e, pl.ds(i * 4, 4)] = total[:, e]
+
+            if o == 2:
+                y_copies[q, "far", 1] = send(summed.at[q, yy, 0], y_relay.at[q, 0], k.at(dy=1))
+                y_copies[q, "far", 3] = send(summed.at[q, yy, 1], y_relay.at[q, 1], k.at(dy=3))
+            elif o:
+                e = 1 if o == 1 else 0
+                y_copies[q, "near", o] = send(
+                    summed.at[q, yy, e], y_recv.at[q, o // 2, e], k.at(dy=o)
+                )
+
+    def y_pass(q):
+        for e, o in ((0, 1), (1, 3)):
+            y_copies[q, "far", o].wait_recv()
+            yy = lax.rem(y + o, 4)
+
+            @pl.loop(0, 4)
+            def _(i):
+                at = pl.ds(i * 8, 8)
+                total = summed[q, yy, e, at].astype(F32) + y_relay[q, e, at].astype(F32)
+                y_relay[q, e, at] = total.astype(BF16)
+
+            y_copies[q, "sum", o] = send(y_relay.at[q, e], y_recv.at[q, o // 2, e], k.at(dy=o))
 
     x_copies = {}
 
     def y_sum(q):
-        for o in (1, 2, 3):
-            y_copies[q, o].wait_recv()
-
-        @pl.loop(0, 8)
-        def _(i):
-            at = pl.ds(i * 4, 4)
-            total = summed[q, y, at].astype(F32)
-            for o in range(3):
-                total += y_recv[q, o, at].astype(F32)
-            acc[pl.ds(i * 128, 128), :] = total.reshape(128, 128)
-
+        for o in (1, 3):
+            y_copies[q, "near", o].wait_recv()
+            y_copies[q, "sum", o].wait_recv()
         for e in range(2):
+
+            @pl.loop(0, 4)
+            def _(i):
+                at = pl.ds(i * 8, 8)
+                total = summed[q, y, e, at].astype(F32)
+                for o in range(2):
+                    total += y_recv[q, o, e, at].astype(F32)
+                acc[pl.ds(e * 512 + i * 128, 128), :] = total.reshape(128, 128)
+
             for b in range(2):
                 for t in range(8):
                     x_send[q, e, b, :, pl.ds(t * 128, 128)] = acc[
-                        pl.ds(e * 16 + t * 2 + b, 32, stride=32), :
+                        pl.ds(e * 512 + t * 2 + b, 32, stride=16), :
                     ].astype(BF16)
         for n, (dh, dl) in enumerate(((1, 1), (1, 0), (0, 1))):
             x_copies[q, n] = send(
@@ -183,61 +202,65 @@
         g_full[1 - xl, z, at] = (x_recv[q, 0].astype(F32) + x_recv[q, 2].astype(F32)).astype(BF16)
         zg[q].start(1, 1)
 
+    def left_split():
+        load_l.wait()
+        split_bf(in_bf.at[1], l_split)
+        l_rows[xl] = l_split[xl]
+        return send(l_split.at[1 - xl], l_rows.at[xl], k.at(dxl=1))
+
+    def moments_split():
+        for n in range(2):
+            load_m[n].wait()
+            for b in range(2):
+                for t in range(8):
+                    mom[n, b, :, pl.ds(t * 128, 128)] = mom_in[
+                        n, pl.ds(t * 2 + b, 64, stride=16), :
+                    ]
+        return send(mom.at[:, 1 - xl], mom_recv, k.at(dxl=1))
+
+    def left_columns():
+        low = lax.broadcasted_iota(jnp.int32, (64, 128), 1) < 64
+        for j in range(2):
+            for zz in range(8):
+                a = l_rows[j, :, pl.ds(zz // 2 * 128, 128)].astype(F32)
+                b = l_rows[j, :, pl.ds((4 + zz // 2) * 128, 128)].astype(F32)
+                if zz % 2:
+                    a = pltpu.roll(a, 64, 1)
+                else:
+                    b = pltpu.roll(b, 64, 1)
+                l_perm[zz, j] = jnp.where(low, a, b).astype(BF16)
+        l_all[:, z] = l_perm[z]
+
+    xt = left_split()
     core_sum(0)
     xq.wait_recv()
     zq.start(1, 1)
     zq.step(1, 0)
+    y_pass(0)
     core_sum(1)
+    xt.wait_recv()
+    left_columns()
     zq.step(1, 1)
-
-    for n in range(2):
-        load_m[n].wait()
-        for b in range(2):
-            for t in range(8):
-                mom[n, b, :, pl.ds(t * 128, 128)] = mom_in[n, pl.ds(t * 2 + b, 64, stride=16), :]
-    xm = send(mom.at[:, 1 - xl], mom_recv, k.at(dxl=1))
+    y_sum(0)
     zq.step(2, 0)
-
-    xt.wait_recv()
-    low = lax.broadcasted_iota(jnp.int32, (64, 128), 1) < 64
-    for j in range(2):
-        for zz in range(8):
-            a = l_rows[j, :, pl.ds(zz // 2 * 128, 128)].astype(F32)
-            b = l_rows[j, :, pl.ds((4 + zz // 2) * 128, 128)].astype(F32)
-            if zz % 2:
-                a = pltpu.roll(a, 64, 1)
-            else:
-                b = pltpu.roll(b, 64, 1)
-            l_perm[zz, j] = jnp.where(low, a, b).astype(BF16)
-    l_copies = []
-    for o in range(1, 8):
-        zz = lax.rem(z + o, 8)
-        l_copies.append(send(l_perm.at[zz], l_all.at[:, z], k.at(dz=o)))
-    l_all[:, z] = l_perm[z]
-
+    y_pass(1)
     zq.step(2, 1)
+    x_sum(0)
     zq.step(3, 0)
-    y_sum(0)
+    y_sum(1)
     zq.step(3, 1)
-    zq.step(4, 0)
-    x_sum(0)
-    zq.step(4, 1)
-    zg[0].step(1, 0)
-    zg[0].step(1, 1)
-    zg[0].step(2, 0)
-    zg[0].step(2, 1)
-    y_sum(1)
-    zg[0].step(3, 0)
-    zg[0].step(3, 1)
+    zg[0].steps(1)
     x_sum(1)
-    zg[0].step(4, 0)
-    zg[0].step(4, 1)
-    for copy in l_copies:
-        copy.wait_recv()
-    l_t[...] = l_all[...].reshape(1024, 128).astype(F32).T.astype(BF16)
-    for s in range(1, 5):
-        zg[1].step(s, 0)
-        zg[1].step(s, 1)
+    xm = moments_split()
+    zg[0].steps(2)
+    zg[1].steps(1)
+    zg[0].steps(3)
+    zg[1].steps(2)
+    zg[0].steps(4)
+    zg[1].steps(3)
+    l_copies = [send(l_perm.at[lax.rem(z + o, 8)], l_all.at[:, z], k.at(dz=o)) for o in range(1, 8)]
+    zq.steps(4)
+    zg[1].steps(4)
 
     def dot(a, b):
         return jnp.dot(a, b, preferred_element_type=F32)
@@ -260,15 +283,14 @@
             n_buf[lax.rem(xl + j, 2), :, cols] = (first / (jnp.sqrt(second) + 1e-8)).astype(BF16)
     normal = n_buf[...].reshape(128, 1024)
     for h in range(H):
-        per = 16 // H
-        for t in range(W // 256):
-            slabs = q_full[...].reshape(1024, 1024)[h * W + t * 256 : h * W + (t + 1) * 256]
-            part = lax.dot_general(normal, slabs, CONTRACT_LAST, preferred_element_type=F32)
-            part = part.astype(BF16).reshape(2, 64, 256)
-            for j in range(2):
-                m_full[h, j, z, :, pl.ds(t * 256, 256)] = part[j]
-        zm[h].start(1, 0)
-        zm[h].start(1, 1)
+        slabs = q_full[...].reshape(1024, 1024)[h * W : (h + 1) * W]
+        part = lax.dot_general(normal, slabs, CONTRACT_LAST, preferred_element_type=F32)
+        part = part.astype(BF16).reshape(2, 64, W)
+        for j in range(2):
+            m_full[h, j, z] = part[j]
+        if h < 2:
+            zm[h].start(1, 0)
+            zm[h].start(1, 1)
 
     xr = send(r_buf.at[1 - xl], r_recv, k.at(dxl=1))
 
@@ -374,29 +396,6 @@
         up_piece[h] = pack[...].astype(BF16)
         gathers[h].begin()
 
-    left_gram()
-    xl_copy = send(pl_buf.at[1 - xl], pl_recv, k.at(dxl=1))
-    zm[0].step(1, 0)
-    zm[0].step(1, 1)
-    zm[1].step(1, 0)
-    zm[1].step(1, 1)
-    right_gram()
-    xr_copy = send(pr_buf.at[1 - xl], pr_recv, k.at(dxl=1))
-    for s in (2, 3):
-        for h in range(H):
-            zm[h].step(s, 0)
-            zm[h].step(s, 1)
-    zm[0].step(4, 0)
-    zm[0].step(4, 1)
-    update(0)
-    zm[1].step(4, 0)
-    zm[1].step(4, 1)
-    pack_up(0)
-    update(1)
-    gathers[0].x_arrive()
-    pack_up(1)
-    gathers[0].relay(0)
-
     def woven(buf, received, b, t):
         cols = pl.ds(t * 128, 128)
         return jnp.where(xl == b, buf[xl, :, cols], received[:, cols])
@@ -416,25 +415,72 @@
                 at = pl.ds(t * 2 + b, 64, stride=16)
                 dst[at, :] = 0.95 * gram_in[n, at, :] + 0.05 * woven(buf, received, b, t)
 
+    left_gram()
+    xl_copy = send(pl_buf.at[1 - xl], pl_recv, k.at(dxl=1))
+    zm[0].steps(1)
+    zm[2].start(1, 0)
+    zm[2].start(1, 1)
+    zm[1].steps(1)
+    zm[3].start(1, 0)
+    zm[3].start(1, 1)
+    right_gram()
+    xr_copy = send(pr_buf.at[1 - xl], pr_recv, k.at(dxl=1))
+    zm[0].steps(2)
+    zm[2].steps(1)
+    zm[1].steps(2)
+    zm[3].steps(1)
+    for copy in l_copies:
+        copy.wait_recv()
+    l_t[...] = l_all[...].reshape(1024, 128).astype(F32).T.astype(BF16)
+    zm[0].steps(3)
+    zm[2].steps(2)
+    zm[1].steps(3)
+    zm[3].steps(2)
+    zm[0].steps(4)
+    update(0)
+    zm[2].steps(3)
+    zm[1].steps(4)
+    update(1)
+    pack_up(0)
+    zm[3].steps(3)
+    zm[2].steps(4)
+    update(2)
+    pack_up(1)
+    zm[3].steps(4)
+    update(3)
+    gathers[0].x_arrive()
+    gathers[0].relay(0)
+    pack_up(2)
+    gathers[1].x_arrive()
+    gathers[1].relay(0)
+    pack_up(3)
     xr.wait_recv()
     new_moments()
     results = [local(new_first, new_first_out), local(new_second, new_second_out)]
-    gathers[1].x_arrive()
+    gathers[0].finish(0)
     gathers[0].relay(1)
-    gathers[0].finish(0)
+    gathers[2].x_arrive()
+    gathers[2].relay(0)
+    gathers[1].finish(0)
+    gathers[1].relay(1)
+    gathers[3].x_arrive()
+    gathers[3].relay(0)
     xl_copy.wait_recv()
     new_gram(new_left, 0, pl_buf, pl_recv)
     results.append(local(new_left, new_left_out))
-    gathers[1].relay(0)
     gathers[0].finish(1)
+    gathers[2].finish(0)
+    gathers[2].relay(1)
+    gathers[1].finish(1)
     xr_copy.wait_recv()
     new_gram(new_right, 1, pr_buf, pr_recv)
     results.append(local(new_right, new_right_out))
-    gathers[1].relay(1)
-    gathers[1].finish(0)
-    gathers[1].finish(1)
-    gathers[0].end()
-    gathers[1].end()
+    gathers[3].finish(0)
+    gathers[3].relay(1)
+    gathers[2].finish(1)
+    gathers[3].finish(1)
+    for gather in gathers:
+        gather.end()
     for copy in results:
         copy.wait()
     for copy in unsent:
@@ -443,6 +489,7 @@
 
 def write_out(part, n1, n2, nl, nr, update, o1, o2, ol, orr, held, whole, rest, sems):
     loads, copies = [], []
+    top = lax.broadcasted_iota(jnp.int32, (8, 8, 128), 1) < 4
     for n in range(4):
         at = pl.ds(n * 4, 4)
         loads.append(pltpu.make_async_copy(part.at[at], held.at[at], sems.at[n]))
@@ -456,11 +503,16 @@
         @pl.loop(n * 4, n * 4 + 4)
         def _(d):
             for r in range(4):
-                rows = [
-                    held[d, h, pl.ds(r * 128, 128), :].astype(F32).reshape(16, 8, 128)
+                a0, a1, a2, a3 = (
+                    held[d, h, pl.ds(r * 64, 64), :].astype(F32).reshape(8, 8, 128)
                     for h in range(H)
-                ]
-                whole[pl.ds(r * 16, 16), d] = jnp.concatenate(rows, axis=1).astype(BF16)
+                )
+                even, odd = [], []
+                for p, q in ((a0, a1), (a2, a3)):
+                    even.append(jnp.where(top, p, pltpu.roll(q, 4, 1)))
+                    odd.append(jnp.where(top, pltpu.roll(p, 4, 1), q))
+                rows = jnp.stack([jnp.concatenate(even, axis=1), jnp.concatenate(odd, axis=1)], axis=1)
+                whole[pl.ds(r * 16, 16), d] = rows.reshape(16, 16, 128).astype(BF16)
 
         at = (slice(None), pl.ds(n * 4, 4))
         copies.append(pltpu.make_async_copy(whole.at[at], update.at[at], sems.at[8 + n]))
@@ -495,8 +547,9 @@
             v((2, 1024, 128), F32),
             v((2, 32, 8, 16, 128), BF16),
             v((2, 32, 8, 16, 128), BF16),
-            v((2, 4, 32, 2, 16, 128), BF16),
-            v((2, 3, 32, 2, 16, 128), BF16),
+            v((2, 4, 2, 32, 16, 128), BF16),
+            v((2, 2, 2, 32, 16, 128), BF16),
+            v((2, 2, 32, 16, 128), BF16),
             v((2, 2, 2, 32, 1024), BF16),
             v((2, 3, 32, 1024), BF16),
             v((1024, 128), F32),

time: 125 us -> 117 us (0.936)
  Pallas kernels: 124 us -> 116 us
    pallas_call x1, Pallas kernels: 119 us -> 111 us  [per_device(): pl.pallas_call(kernel, out_shape=[shape((16, H, PIECE, 128), BF16)] + [sh...]
where the time goes in v3:
time: 117 us
  Pallas kernels  116 us (99%)
    pallas_call x1, Pallas kernels, per_device(): pl.pallas_call(kernel, out_shape=[shape((16, H, PIECE, 128), BF16)] + [sh...  111 us
    pallas_call x1, Pallas kernels, per_device(): pl.pallas_call(write_out, out_shape=[shape((64, 16, 16, 128), BF16)] + [s...  4.64 us

profile of v3, /device:TPU:1, one launch (start us, length us, event | category | flops | bytes accessed | tf_op | source)
XLA Modules:
  0.0 116.7 jit_solution(8437663587028689497)
XLA Ops:
  0.6 111.4 %soap.1 = (bf16[16,4,256,128]{3,2,1,0:T(8,128)(2,1)}, f32[1024,128]{1,0:T(8,128)}, f32[1024,128]{1,0:T(8,128)}, f32[1024,128]{1,0:T(8,128)}, f32[1024,128]{1,0:T(8,128)}) custom-call(bf16[64,8,2,16,128]{4,3,2,1,0:T(8,128)(2,1)} %bitcast.60, bf16[64,16,128]{2,1,0:T(8,128)(2,1)} %bitcast.65, bf16[64,16,128]{2,1,0:T(8,128)(2,1)} %bitcast.66, ...), custom_call_target="tpu_custom_call" | custom-call | tf_op jit(solution)/shard_map/soap/pallas_call | solution.py:535
  112.1 4.6 %write_out.1 = (bf16[64,16,16,128]{3,2,1,0:T(8,128)(2,1)}, f32[1024,128]{1,0:T(8,128)}, f32[1024,128]{1,0:T(8,128)}, f32[1024,128]{1,0:T(8,128)}, f32[1024,128]{1,0:T(8,128)}) custom-call(bf16[16,4,256,128]{3,2,1,0:T(8,128)(2,1)} %get-tuple-element.15.part, f32[1024,128]{1,0:T(8,128)} %get-tuple-element.16.n1, f32[1024,128]{1,0:T(8,128)} %get-tuple-element.17.n2, ...), custom_call_target="tpu_custom_call" | custom-call | tf_op jit(solution)/shard_map/write_out/pallas_call | solution.py:589

commit v4 on v3

--- a/solution.py
+++ b/solution.py
@@ -37,7 +37,7 @@
     new_first, new_second, new_left, new_right, gram_in, in_bf, mom_in, own, other, summed, y_recv, y_relay, x_send, x_recv, acc,
     q_split, q_full, l_split, l_rows, l_perm, l_all, l_t,
     g_full, mom, mom_recv, y_rot, n_buf, m_full, r_buf, r_recv, pl_buf, pl_recv, pr_buf, pr_recv,
-    g_cols, up_send, up_recv, pack, up_piece,
+    ret, g_cols, up_send, up_recv, pack, up_piece,
     ss, rs, ls,
 ):
     k = Peers()
@@ -77,7 +77,21 @@
 
     load_q = local(qr, in_bf.at[0])
     load_l = local(lt, in_bf.at[1])
-    load_own = [local(g.at[pl.ds(q * 32, 32), :, c], own.at[q]) for q in range(2)]
+    def pairs(q, o):
+        two = pl.ds(lax.rem(y + o, 4) * 2, 2)
+        rows = pl.ds(q * 32, 32)
+        return [g.at[rows, two, cc] for cc in (c, 1 - c)], (q, slice(None), two)
+
+    def load_pair(q, o):
+        (mine, _), at = pairs(q, o)
+        return local(mine, own.at[at])
+
+    def swap_pair(q, o):
+        (_, theirs), at = pairs(q, o)
+        return send(theirs, other.at[at], k.at(dc=1))
+
+    order = (2, 1, 3, 0)
+    load_own = {(q, o): load_pair(q, o) for q in range(2) for o in order}
     load_m = [local(m1, mom_in.at[0]), local(m2, mom_in.at[1])]
     load_g = [local(lg, gram_in.at[0]), local(rg, gram_in.at[1])]
 
@@ -88,15 +102,16 @@
                 dst[b, :, pl.ds(t * 128, 128)] = acc[pl.ds(t * 2 + b, 64, stride=16), :].astype(BF16)
 
     class ZGather:
-        def __init__(self, ref):
-            self.ref, self.copies = ref, {}
+        def __init__(self, ref, skip=False):
+            self.ref, self.copies, self.skip = ref, {}, skip
 
         def start(self, s, j):
             for d in (1, -1):
                 if s == 4 and j != (d == -1):
                     continue
-                at = self.ref(lax.rem(xl + j, 2), lax.rem(z - d * (s - 1) + 8, 8))
-                self.copies[s, j, d] = send(at, at, k.at(dz=d % 8))
+                back, on = (2, 2) if s == 4 and self.skip else (s - 1, 1)
+                at = self.ref(lax.rem(xl + j, 2), lax.rem(z - d * back + 8, 8))
+                self.copies[s, j, d] = send(at, at, k.at(dz=d * on % 8))
 
         def arrive(self, s, j):
             for d in (1, -1):
@@ -105,8 +120,10 @@
 
         def step(self, s, j):
             self.arrive(s, j)
-            if s < 4:
+            if s < 3 or s == 3 and not self.skip:
                 self.start(s + 1, j)
+            if s == 2 and self.skip:
+                self.start(4, j)
 
         def steps(self, s):
             self.step(s, 0)
@@ -114,23 +131,47 @@
 
     zq = ZGather(lambda j, zz: q_full.at[j, zz])
     zg = [
-        ZGather(lambda j, zz, q=q: g_full.at[j, zz, pl.ds(q * 32, 32), :]) for q in range(2)
+        ZGather(lambda j, zz, q=q: g_full.at[j, zz, pl.ds(q * 32, 32), :], q == 1) for q in range(2)
     ]
-    zm = [ZGather(lambda j, zz, h=h: m_full.at[h, j, zz]) for h in range(H)]
-
-    pl.semaphore_wait(barrier, len(partners))
-    core = [send(g.at[pl.ds(q * 32, 32), :, 1 - c], other.at[q], k.at(dc=1)) for q in range(2)]
+    zm = [ZGather(lambda j, zz, h=h: m_full.at[h, j, zz], False) for h in range(H)]
+
+    def left_columns(j):
+        low = lax.broadcasted_iota(jnp.int32, (64, 128), 1) < 64
+        for zz in range(8):
+            a = l_rows[j, :, pl.ds(zz // 2 * 128, 128)].astype(F32)
+            b = l_rows[j, :, pl.ds((4 + zz // 2) * 128, 128)].astype(F32)
+            if zz % 2:
+                a = pltpu.roll(a, 64, 1)
+            else:
+                b = pltpu.roll(b, 64, 1)
+            l_perm[zz, j] = jnp.where(low, a, b).astype(BF16)
+        l_all[j, z] = l_perm[z, j]
+
+    def left_send(j):
+        return [
+            send(l_perm.at[lax.rem(z + o, 8), j], l_all.at[j, z], k.at(dz=o))
+            for o in (1, 7, 2, 6, 3, 5, 4)
+        ]
+
     load_q.wait()
     split_bf(in_bf.at[0], q_split)
     q_full[xl, z] = q_split[xl]
+    load_l.wait()
+    split_bf(in_bf.at[1], l_split)
+    l_rows[xl] = l_split[xl]
+    left_columns(xl)
+    pl.semaphore_wait(barrier, len(partners))
+    core = {(0, o): swap_pair(0, o) for o in order}
+    zq.start(1, 0)
     xq = send(q_split.at[1 - xl], q_full.at[xl, z], k.at(dxl=1))
-    zq.start(1, 0)
+    xt = send(l_split.at[1 - xl], l_rows.at[xl], k.at(dxl=1))
+    l_copies = left_send(xl)
     y_copies = {}
 
     def core_sum(q):
-        load_own[q].wait()
-        core[q].wait_recv()
-        for o in (2, 1, 3, 0):
+        for o in order:
+            load_own[q, o].wait()
+            core[q, o].wait_recv()
             yy = lax.rem(y + o, 4)
 
             @pl.loop(0, 8)
@@ -202,12 +243,6 @@
         g_full[1 - xl, z, at] = (x_recv[q, 0].astype(F32) + x_recv[q, 2].astype(F32)).astype(BF16)
         zg[q].start(1, 1)
 
-    def left_split():
-        load_l.wait()
-        split_bf(in_bf.at[1], l_split)
-        l_rows[xl] = l_split[xl]
-        return send(l_split.at[1 - xl], l_rows.at[xl], k.at(dxl=1))
-
     def moments_split():
         for n in range(2):
             load_m[n].wait()
@@ -218,28 +253,15 @@
                     ]
         return send(mom.at[:, 1 - xl], mom_recv, k.at(dxl=1))
 
-    def left_columns():
-        low = lax.broadcasted_iota(jnp.int32, (64, 128), 1) < 64
-        for j in range(2):
-            for zz in range(8):
-                a = l_rows[j, :, pl.ds(zz // 2 * 128, 128)].astype(F32)
-                b = l_rows[j, :, pl.ds((4 + zz // 2) * 128, 128)].astype(F32)
-                if zz % 2:
-                    a = pltpu.roll(a, 64, 1)
-                else:
-                    b = pltpu.roll(b, 64, 1)
-                l_perm[zz, j] = jnp.where(low, a, b).astype(BF16)
-        l_all[:, z] = l_perm[z]
-
-    xt = left_split()
     core_sum(0)
+    core.update({(1, o): swap_pair(1, o) for o in order})
     xq.wait_recv()
     zq.start(1, 1)
     zq.step(1, 0)
     y_pass(0)
     core_sum(1)
     xt.wait_recv()
-    left_columns()
+    left_columns(1 - xl)
     zq.step(1, 1)
     y_sum(0)
     zq.step(2, 0)
@@ -258,7 +280,7 @@
     zg[1].steps(2)
     zg[0].steps(4)
     zg[1].steps(3)
-    l_copies = [send(l_perm.at[lax.rem(z + o, 8)], l_all.at[:, z], k.at(dz=o)) for o in range(1, 8)]
+    l_copies += left_send(1 - xl)
     zq.steps(4)
     zg[1].steps(4)
 
@@ -292,7 +314,8 @@
             zm[h].start(1, 0)
             zm[h].start(1, 1)
 
-    xr = send(r_buf.at[1 - xl], r_recv, k.at(dxl=1))
+    ret[0] = r_buf[1 - xl].astype(BF16)
+    xr = send(ret.at[0], r_recv, k.at(dxl=1))
 
     def left_gram():
         rows = g_full[:, z].reshape(128, 1024)
@@ -382,7 +405,33 @@
                     self.got[e, o, "c"].wait_recv()
             self.keep.wait()
 
-    gathers = [Gather(h) for h in range(H)]
+    class GatherYFirst(Gather):
+        def begin(self):
+            self.keep = local(up_piece.at[self.h], self.place(0, 0, 0))
+            self.push((0, 1), None, k.at(dy=1))
+            self.push((0, 3), None, k.at(dy=3))
+            self.push((0, "x"), None, k.at(dxh=1))
+            self.push((0, 0, "c"), None, k.at(dc=1))
+
+        def relay(self, e):
+            for o, half in ((1, 0), (3, 1)):
+                self.got[0, o].wait_recv()
+                self.push((0, 2, half), self.place(4 - o, 0, 0, half), k.at(dy=o))
+                self.push((o, "x"), self.place(4 - o, 0, 0), k.at(dxh=1))
+                self.push((0, o, "c"), self.place(4 - o, 0, 0), k.at(dc=1))
+
+        def finish(self, e):
+            for half in range(2):
+                self.got[0, 2, half].wait_recv()
+            self.push((2, "x"), self.place(2, 0, 0), k.at(dxh=1))
+            self.push((0, 2, "c"), self.place(2, 0, 0), k.at(dc=1))
+
+        def x_arrive(self, steps):
+            for o in steps:
+                self.got[o, "x"].wait_recv()
+                self.push((1, o, "c"), self.place(4 - o if o else 0, 1, 0), k.at(dc=1))
+
+    gathers = [GatherYFirst(0)] + [Gather(h) for h in range(1, H)]
 
     def pack_up(h):
         up_copies[h].wait_recv()
@@ -398,7 +447,7 @@
 
     def woven(buf, received, b, t):
         cols = pl.ds(t * 128, 128)
-        return jnp.where(xl == b, buf[xl, :, cols], received[:, cols])
+        return jnp.where(xl == b, buf[xl, :, cols], received[:, cols].astype(F32))
 
     def new_moments():
         for b in range(2):
@@ -416,7 +465,8 @@
                 dst[at, :] = 0.95 * gram_in[n, at, :] + 0.05 * woven(buf, received, b, t)
 
     left_gram()
-    xl_copy = send(pl_buf.at[1 - xl], pl_recv, k.at(dxl=1))
+    ret[1] = pl_buf[1 - xl].astype(BF16)
+    xl_copy = send(ret.at[1], pl_recv, k.at(dxl=1))
     zm[0].steps(1)
     zm[2].start(1, 0)
     zm[2].start(1, 1)
@@ -424,7 +474,8 @@
     zm[3].start(1, 0)
     zm[3].start(1, 1)
     right_gram()
-    xr_copy = send(pr_buf.at[1 - xl], pr_recv, k.at(dxl=1))
+    ret[2] = pr_buf[1 - xl].astype(BF16)
+    xr_copy = send(ret.at[2], pr_recv, k.at(dxl=1))
     zm[0].steps(2)
     zm[2].steps(1)
     zm[1].steps(2)
@@ -448,7 +499,6 @@
     pack_up(1)
     zm[3].steps(4)
     update(3)
-    gathers[0].x_arrive()
     gathers[0].relay(0)
     pack_up(2)
     gathers[1].x_arrive()
@@ -458,20 +508,21 @@
     new_moments()
     results = [local(new_first, new_first_out), local(new_second, new_second_out)]
     gathers[0].finish(0)
-    gathers[0].relay(1)
+    gathers[0].x_arrive((0,))
     gathers[2].x_arrive()
     gathers[2].relay(0)
     gathers[1].finish(0)
     gathers[1].relay(1)
     gathers[3].x_arrive()
     gathers[3].relay(0)
+    gathers[0].x_arrive((1, 3))
     xl_copy.wait_recv()
     new_gram(new_left, 0, pl_buf, pl_recv)
     results.append(local(new_left, new_left_out))
-    gathers[0].finish(1)
     gathers[2].finish(0)
     gathers[2].relay(1)
     gathers[1].finish(1)
+    gathers[0].x_arrive((2,))
     xr_copy.wait_recv()
     new_gram(new_right, 1, pr_buf, pr_recv)
     results.append(local(new_right, new_right_out))
@@ -567,11 +618,12 @@
             v((2, 64, 1024), BF16),
             v((H, 2, 8, 64, W), BF16),
             v((2, 64, 1024), F32),
-            v((64, 1024), F32),
+            v((64, 1024), BF16),
             v((2, 64, 1024), F32),
-            v((64, 1024), F32),
+            v((64, 1024), BF16),
             v((2, 64, 1024), F32),
-            v((64, 1024), F32),
+            v((64, 1024), BF16),
+            v((3, 64, 1024), BF16),
             v((128, 1024), BF16),
             v((H, 2, 64, W), BF16),
             v((H, 64, W), BF16),
@@ -579,7 +631,7 @@
             v((H, PIECE, 128), BF16),
             pltpu.SemaphoreType.DMA((NCOPY,)),
             pltpu.SemaphoreType.DMA((NCOPY,)),
-            pltpu.SemaphoreType.DMA((16,)),
+            pltpu.SemaphoreType.DMA((24,)),
         ],
         compiler_params=pltpu.CompilerParams(
             collective_id=0, has_side_effects=True, vmem_limit_bytes=56 << 20

time: 117 us -> 113 us (0.966)
  Pallas kernels: 116 us -> 113 us
    pallas_call x1, Pallas kernels: 111 us -> 108 us  [per_device(): pl.pallas_call(kernel, out_shape=[shape((16, H, PIECE, 128), BF16)] + [sh...]
where the time goes in v4:
time: 113 us
  Pallas kernels  113 us (100%)
    pallas_call x1, Pallas kernels, per_device(): pl.pallas_call(kernel, out_shape=[shape((16, H, PIECE, 128), BF16)] + [sh...  108 us
    pallas_call x1, Pallas kernels, per_device(): pl.pallas_call(write_out, out_shape=[shape((64, 16, 16, 128), BF16)] + [s...  4.64 us

profile of v4, /device:TPU:1, one launch (start us, length us, event | category | flops | bytes accessed | tf_op | source)
XLA Modules:
  0.0 113.3 jit_solution(10328963037476803733)
XLA Ops:
  0.6 108.1 %soap.1 = (bf16[16,4,256,128]{3,2,1,0:T(8,128)(2,1)}, f32[1024,128]{1,0:T(8,128)}, f32[1024,128]{1,0:T(8,128)}, f32[1024,128]{1,0:T(8,128)}, f32[1024,128]{1,0:T(8,128)}) custom-call(bf16[64,8,2,16,128]{4,3,2,1,0:T(8,128)(2,1)} %bitcast.60, bf16[64,16,128]{2,1,0:T(8,128)(2,1)} %bitcast.65, bf16[64,16,128]{2,1,0:T(8,128)(2,1)} %bitcast.66, ...), custom_call_target="tpu_custom_call" | custom-call | tf_op jit(solution)/shard_map/soap/pallas_call | solution.py:586
  108.7 4.6 %write_out.1 = (bf16[64,16,16,128]{3,2,1,0:T(8,128)(2,1)}, f32[1024,128]{1,0:T(8,128)}, f32[1024,128]{1,0:T(8,128)}, f32[1024,128]{1,0:T(8,128)}, f32[1024,128]{1,0:T(8,128)}) custom-call(bf16[16,4,256,128]{3,2,1,0:T(8,128)(2,1)} %get-tuple-element.15.part, f32[1024,128]{1,0:T(8,128)} %get-tuple-element.16.n1, f32[1024,128]{1,0:T(8,128)} %get-tuple-element.17.n2, ...), custom_call_target="tpu_custom_call" | custom-call | tf_op jit(solution)/shard_map/write_out/pallas_call | solution.py:641

commit v5 on v4

--- a/solution.py
+++ b/solution.py
@@ -280,7 +280,6 @@
     zg[1].steps(2)
     zg[0].steps(4)
     zg[1].steps(3)
-    l_copies += left_send(1 - xl)
     zq.steps(4)
     zg[1].steps(4)
 
@@ -314,6 +313,7 @@
             zm[h].start(1, 0)
             zm[h].start(1, 1)
 
+    l_copies += left_send(1 - xl)
     ret[0] = r_buf[1 - xl].astype(BF16)
     xr = send(ret.at[0], r_recv, k.at(dxl=1))
 
@@ -389,9 +389,9 @@
         def relay(self, e):
             self.got[e, 1].wait_recv()
             self.push((e, 2, 0), self.place(3, e, 0, 0), k.at(dy=1))
-            self.push((e, 1, "c"), self.place(3, e, 0), k.at(dc=1))
             self.got[e, 3].wait_recv()
             self.push((e, 2, 1), self.place(1, e, 0, 1), k.at(dy=3))
+            self.push((e, 1, "c"), self.place(3, e, 0), k.at(dc=1))
             self.push((e, 3, "c"), self.place(1, e, 0), k.at(dc=1))
 
         def finish(self, e):

time: 113 us -> 115 us (1.018)
  no operation moved by 1% of the time
where the time goes in v5:
time: 115 us; the launch traced here: 114 us
  Pallas kernels  114 us (99%)
    pallas_call x1, Pallas kernels, per_device(): pl.pallas_call(kernel, out_shape=[shape((16, H, PIECE, 128), BF16)] + [sh...  109 us
    pallas_call x1, Pallas kernels, per_device(): pl.pallas_call(write_out, out_shape=[shape((64, 16, 16, 128), BF16)] + [s...  4.64 us

profile of v5, /device:TPU:1, one launch (start us, length us, event | category | flops | bytes accessed | tf_op | source)
XLA Modules:
  0.0 114.5 jit_solution(6932846811057424658)
XLA Ops:
  0.6 109.2 %soap.1 = (bf16[16,4,256,128]{3,2,1,0:T(8,128)(2,1)}, f32[1024,128]{1,0:T(8,128)}, f32[1024,128]{1,0:T(8,128)}, f32[1024,128]{1,0:T(8,128)}, f32[1024,128]{1,0:T(8,128)}) custom-call(bf16[64,8,2,16,128]{4,3,2,1,0:T(8,128)(2,1)} %bitcast.60, bf16[64,16,128]{2,1,0:T(8,128)(2,1)} %bitcast.65, bf16[64,16,128]{2,1,0:T(8,128)(2,1)} %bitcast.66, ...), custom_call_target="tpu_custom_call" | custom-call | tf_op jit(solution)/shard_map/soap/pallas_call | solution.py:586
  109.8 4.6 %write_out.1 = (bf16[64,16,16,128]{3,2,1,0:T(8,128)(2,1)}, f32[1024,128]{1,0:T(8,128)}, f32[1024,128]{1,0:T(8,128)}, f32[1024,128]{1,0:T(8,128)}, f32[1024,128]{1,0:T(8,128)}) custom-call(bf16[16,4,256,128]{3,2,1,0:T(8,128)(2,1)} %get-tuple-element.15.part, f32[1024,128]{1,0:T(8,128)} %get-tuple-element.16.n1, f32[1024,128]{1,0:T(8,128)} %get-tuple-element.17.n2, ...), custom_call_target="tpu_custom_call" | custom-call | tf_op jit(solution)/shard_map/write_out/pallas_call | solution.py:641
